TPU v7x, 32 devices: a whole 2x2x4 slice. The times are simulated.
32 devices in a mesh: grp: 2 (over x), sfc: 16 (over z, y, core).
Axes of the slice: x: 2, y: 2, z: 4, core: 2. Of those that a mesh axis runs over, the one named last changes fastest.
Arguments:
- tracers: float32 [8, 64, 16384], P(None, None, ('grp', 'sfc')), parts along dimension 2, may hold values from -6 to 6
- velocity: float32 [2, 64, 16384], P(None, None, ('grp', 'sfc')), parts along dimension 2, may hold values from -4 to 4
- metric: float32 [16384], P(('grp', 'sfc')), parts along dimension 0, may hold values from 0.5 to 2
- absorber: bfloat16 [16384, 256], P(('grp', 'sfc')), parts along dimension 0, may hold values from 0.049804688 to 1
- cosine_zenith: bfloat16 [16384], P(('grp', 'sfc')), parts along dimension 0, may hold values from 0.049804688 to 1
- layer_mass: bfloat16 [64, 16384], P(None, ('grp', 'sfc')), parts along dimension 1, may hold values from 0.5 to 2
- absorption: bfloat16 [4, 112, 64], replicated, may hold values from 0.0009994507 to 0.29882812
- solar_flux: float32 [112], replicated, may hold values from 0.1 to 1
- sunlit: int32 [128], P(('grp', 'sfc')), parts along dimension 0, may hold values from 0 to 1, as said below
- neighbour: int32 [4, 1024], P(None, ('grp', 'sfc')), parts along dimension 1, may hold values from 0 to 511, as said below
- neighbour_edge: int32 [4, 1024], P(None, ('grp', 'sfc')), parts along dimension 1, may hold values from 0 to 3
Outputs:
- advanced: float32 [8, 64, 16384], P(None, None, ('grp', 'sfc')), parts along dimension 2
- heating: float32 [64, 16384], P(None, ('grp', 'sfc')), parts along dimension 1
There are 2 independent parts, one for each index of `grp`. A program takes and returns all parts, laid end to end along the dimension named above; an argument that names none is the same for every part. Nothing has to cross between parts.
Inputs may be any that keep to these rules, and one draw needn't show every extreme that they name: `sunlit`: the 1s form one cyclic run of 32 consecutive blocks; all other blocks are 0. For an element among the 32 elements of device position d along sfc (elements d * 32 to (d + 1) * 32 - 1), every neighbour lies among those elements or the 8 elements on either side of them, counted cyclically over 512; on every device both ends of that range are named.
All inputs are finite; a program needn't handle non-finite values.
Results may differ from a plain program's by a relative error of at most 0.0003.
Values may be sent and summed in bfloat16 or wider, within the bound.
No kernel may reach another device: no remote copies, remote signals or barrier semaphores. Data moves between devices by JAX's collectives and lax.ppermute only.
A program may use at most 64 MiB of HBM per device.

v0:
```python
import functools
import math

import jax
import jax.numpy as jnp
import numpy as np
from jax import lax
from jax.experimental import pallas as pl
from jax.experimental.pallas import tpu as pltpu
from jax.sharding import PartitionSpec as P

BLOCK = 128
RIM = 8
STEP = 0.1
BITS = 21
LOWER = 32 - BITS
HALF = 1 << (BITS - 1)
SPAN = float(HALF - 8)
F32 = jnp.float32
BF16 = jnp.bfloat16
VMEM = pl.BlockSpec(memory_space=pltpu.VMEM)
SMEM = pl.BlockSpec(memory_space=pltpu.SMEM)
HBM = pl.BlockSpec(memory_space=pltpu.HBM)


def derivative_table():
    nodes = np.array([-1.0, -1.0 / math.sqrt(5.0), 1.0 / math.sqrt(5.0), 1.0])
    weights = np.array(
        [1.0 / np.prod([nodes[i] - nodes[m] for m in range(4) if m != i]) for i in range(4)]
    )
    table = np.zeros((4, 4))
    for i in range(4):
        for m in range(4):
            if i != m:
                table[i, m] = weights[m] / weights[i] / (nodes[i] - nodes[m])
        table[i, i] = -sum(table[i, m] for m in range(4) if m != i)
    return table


def params(mib=8):
    return pltpu.CompilerParams(vmem_limit_bytes=mib << 20)


def cost(flops, size=1 << 20):
    return pl.CostEstimate(flops=int(flops), bytes_accessed=int(size), transcendentals=0)


def iota(shape, dim):
    return lax.broadcasted_iota(jnp.int32, shape, dim)


def split(x):
    high = x.astype(BF16)
    return high, (x - high.astype(F32)).astype(BF16)


def dot(a, b):
    return jnp.dot(a, b, preferred_element_type=F32)


def build_derivatives(wide_ref, fine_ref):
    table = derivative_table()
    src, dst = iota((BLOCK, BLOCK), 0), iota((BLOCK, BLOCK), 1)
    si, sj, di, dj = src // 4 % 4, src % 4, dst // 4 % 4, dst % 4
    same = src // 16 == dst // 16
    halves = []
    for d, s, keep in ((di, si, same & (sj == dj)), (dj, sj, same & (si == di))):
        pick = jnp.where(keep, d * 4 + s, -1)
        value = jnp.zeros((BLOCK, BLOCK), F32)
        for i in range(4):
            for m in range(4):
                value = jnp.where(pick == i * 4 + m, float(table[i, m]), value)
        halves.append(value)
    high, low = split(jnp.concatenate(halves, axis=1))
    wide_ref[:BLOCK] = high
    wide_ref[BLOCK:] = high
    fine_ref[...] = low


def advance(field, first, second, wide_ref, fine_ref):
    high, low = split(field)
    both = dot(jnp.concatenate([high, low], axis=1), wide_ref[...]) + dot(high, fine_ref[...])
    return field + first * both[:, :BLOCK] + second * both[:, BLOCK:]


def repeat_rows(x, times):
    return jnp.concatenate([x] * times, axis=0) if times > 1 else x


def rim_starts(cols):
    near = jnp.where(lax.axis_index("sfc") % 2 == 0, cols - BLOCK, 0)
    return pl.multiple_of(near, BLOCK), pl.multiple_of(cols - BLOCK - near, BLOCK)


def rim_kernel(levels, *refs):
    count = (len(refs) - 5) // 2
    given, (sent, far, wide, fine), kept, sems = (
        refs[:count], refs[count : count + 4], refs[count + 4 : -1], refs[-1],
    )
    tr_hbm, vel_hbm, metric_hbm = given[:3]
    tr, vel, metric = kept[:3]
    rows, cols = tr.shape
    rims = [pl.ds(start, BLOCK) for start in rim_starts(cols)[::-1]]
    inner = pl.ds(BLOCK, cols - 2 * BLOCK)
    pairs = [(metric_hbm, metric)]
    pairs += [(hbm.at[:, r], ref.at[:, r]) for r in rims for hbm, ref in ((vel_hbm, vel), (tr_hbm, tr))]
    pairs += [(hbm.at[:, inner], ref.at[:, inner]) for hbm, ref in ((vel_hbm, vel), (tr_hbm, tr))]
    pairs += list(zip(given[3:], kept[3:], strict=True))
    copies = [pltpu.make_async_copy(a, b, sems.at[k]) for k, (a, b) in enumerate(pairs)]
    for copy in copies:
        copy.start()
    build_derivatives(wide, fine)
    copies[0].wait()
    for copy in copies[1:3]:
        copy.wait()
    rim = rims[0]
    scale = -STEP * metric[:, rim]
    first = repeat_rows(vel[:levels, rim] * scale, rows // levels)
    second = repeat_rows(vel[levels:, rim] * scale, rows // levels)
    field = advance(tr[:, rim], first, second, wide, fine)
    far[...] = field
    sent[...] = encode(field)
    for copy in copies[3:]:
        copy.wait()


def is_point(shape, *points):
    point = iota(shape, 1) % 16
    return functools.reduce(jnp.logical_or, [point == p for p in points])


def shifted(x, shift):
    return pltpu.roll(x, shift % BLOCK, 1)


def pack(rim):
    size = rim.shape[0] // 4
    a, b, c, d = (rim[k * size : (k + 1) * size] for k in range(4))
    shape = d.shape
    upper = is_point(shape, 5, 6)
    moved = (
        jnp.where(upper, shifted(d, 5), shifted(d, 7)),
        jnp.where(upper, shifted(d, -7), shifted(d, -5)),
        jnp.where(is_point(shape, 5, 9), shifted(d, 1), shifted(d, -1)),
    )
    inside = is_point(shape, 5, 6, 9, 10)
    return jnp.concatenate([jnp.where(inside, m, x) for m, x in zip(moved, (a, b, c), strict=True)], axis=0)


def encode(rim):
    packed = pack(rim)
    strips = [packed[r : r + 8] for r in range(0, packed.shape[0], 8)]
    largest = functools.reduce(jnp.maximum, [jnp.abs(x) for x in strips])
    power = jnp.clip(jnp.ceil(jnp.log2(largest)), -125.0, 125.0)
    scale = jnp.exp2(-power)
    count = len(strips) // 3
    words = [(x * scale * SPAN + (HALF + 0.5)).astype(jnp.int32) for x in strips]
    a, b, c = (words[k * count : (k + 1) * count] for k in range(3))
    first = [x | (z << BITS) for x, z in zip(a, c, strict=True)]
    second = [y | ((z >> LOWER) << BITS) for y, z in zip(b, c, strict=True)]
    return jnp.concatenate([power.astype(jnp.int32)] + first + second, axis=0)


def decode(sent):
    scale = jnp.exp2(sent[:8].astype(F32)) * (1.0 / SPAN)
    count = (sent.shape[0] - 8) // 16
    words = [sent[8 + r * 8 : 16 + r * 8] for r in range(2 * count)]
    a, b, c = [], [], []
    for first, second in zip(words[:count], words[count:], strict=True):
        a.append(first & (2 * HALF - 1))
        b.append(second & (2 * HALF - 1))
        upper = lax.shift_right_logical(second, BITS) << LOWER
        c.append(lax.shift_right_logical(first, BITS) | upper)
    return unpack(jnp.concatenate([(x - HALF).astype(F32) * scale for x in a + b + c], axis=0))


def unpack(sent):
    size = sent.shape[0] // 3
    a, b, c = (sent[k * size : (k + 1) * size] for k in range(3))
    shape = a.shape
    d = jnp.where(is_point(shape, 4, 8), shifted(c, -1), shifted(c, 1))
    d = jnp.where(is_point(shape, 0, 1), shifted(a, -5), d)
    d = jnp.where(is_point(shape, 2, 3), shifted(a, -7), d)
    d = jnp.where(is_point(shape, 12, 13), shifted(b, 7), d)
    d = jnp.where(is_point(shape, 14, 15), shifted(b, 5), d)
    return jnp.concatenate([a, b, c, d], axis=0)


def build_assembly(total, position, nb, ne, local, halo):
    elems, cols = nb.shape[1], local.shape[1]
    index = nb[...] - position * elems + RIM
    index = jnp.where(index < 0, index + total, index)
    index = jnp.where(index >= total, index - total, index)
    code = (index * 4 + ne[...]).astype(F32).astype(BF16)
    spread = (iota((elems, cols), 1) // 16 == iota((elems, cols), 0)).astype(F32).astype(BF16)
    code = dot(code, spread).astype(jnp.int32)
    lane = iota((1, cols), 1)
    i, j = lane // 4 % 4, lane % 4

    def source(code, p):
        edge, q = code % 4, 3 - p
        si = jnp.where(edge == 0, 0, jnp.where(edge == 1, q, jnp.where(edge == 2, 3, 3 - q)))
        sj = jnp.where(edge == 0, q, jnp.where(edge == 1, 3, jnp.where(edge == 2, 3 - q, 0)))
        return code // 4 * 16 + si * 4 + sj

    across = jnp.where(i == 0, source(code[0:1], j), source(code[2:3], 3 - j))
    across = jnp.where((i == 0) | (i == 3), across, -1)
    along = jnp.where(j == 3, source(code[1:2], i), source(code[3:4], 3 - i))
    along = jnp.where((j == 0) | (j == 3), along, -1)
    own = 1.0 - 0.5 * ((across >= 0).astype(F32) + (along >= 0).astype(F32))

    def rows_of(start):
        row = iota((BLOCK, cols), 0) + start
        return jnp.where(row == across, 0.5, 0.0) + jnp.where(row == along, 0.5, 0.0)

    even = position % 2 == 0
    halo[:BLOCK] = rows_of(jnp.where(even, BLOCK + cols, 0)).astype(BF16)
    halo[BLOCK:] = rows_of(jnp.where(even, 0, BLOCK + cols)).astype(BF16)
    for r in range(0, cols, BLOCK):
        value = rows_of(BLOCK + r) + jnp.where(iota((BLOCK, cols), 0) + r == lane, own, 0.0)
        local[r : r + BLOCK] = value.astype(BF16)


def first_kernel(
    total, levels, tr, vel, metric, wide, fine, far, nb, ne,
    sent, part, speed, local, halo, high, low,
):
    rows, cols = tr.shape
    scale = -STEP * metric[...]
    speed[...] = vel[...] * scale
    near_start, far_start = rim_starts(cols)
    for start in (near_start, *range(BLOCK, cols - BLOCK, BLOCK)):
        tile = pl.ds(start, BLOCK)
        first = repeat_rows(speed[:levels, tile], rows // levels)
        second = repeat_rows(speed[levels:, tile], rows // levels)
        field = advance(tr[:, tile], first, second, wide, fine)
        if start is near_start:
            sent[...] = encode(field)
        high[:, tile], low[:, tile] = split(field)
    tile = pl.ds(far_start, BLOCK)
    high[:, tile], low[:, tile] = split(far[...])
    build_assembly(total, lax.axis_index("sfc"), nb, ne, local, halo)
    part[...] = dot(high[...], local[...]) + dot(low[...], local[...])


def halo_parts(near, far):
    nh, nl = split(near)
    fh, fl = split(far)
    return jnp.concatenate([nh, fh], axis=1), jnp.concatenate([nl, fl], axis=1)


def second_rim(levels, start, part, high, low, halo, wide, fine, tr, speed, heat):
    rows, cols = part.shape
    tile = pl.ds(start, BLOCK)
    warm_tile = pl.ds(pl.multiple_of(jnp.where(start == 0, 0, BLOCK), BLOCK), BLOCK)
    section = part[:, tile] + dot(high[...], halo[:, tile]) + dot(low[...], halo[:, tile])
    first = repeat_rows(speed[:levels, tile], rows // levels)
    second = repeat_rows(speed[levels:, tile], rows // levels)
    field = 0.5 * (tr[:, tile] + advance(section, first, second, wide, fine))
    warm = (0.5 * STEP) * heat[:, warm_tile]
    return jnp.concatenate([field[:levels] + warm, field[levels:]], axis=0)


def far2_kernel(
    levels, part, near, sent, halo, wide, fine, tr, speed, heat, out_sent, out_far, high, low
):
    high[...], low[...] = halo_parts(decode(near[...]), decode(sent[...]))
    start = rim_starts(part.shape[1])[1]
    field = second_rim(levels, start, part, high, low, halo, wide, fine, tr, speed, heat)
    out_far[...] = field
    out_sent[...] = encode(field)


def near2_kernel(levels, part, high, low, halo, wide, fine, tr, speed, heat, sent, out):
    start = rim_starts(part.shape[1])[0]
    out[...] = second_rim(levels, start, part, high, low, halo, wide, fine, tr, speed, heat)
    sent[...] = encode(out[...])


def inner2_kernel(
    levels, part, high, low, halo, local, wide, fine, tr, speed, heat,
    own_near, own_far, out, own_high, own_low,
):
    rows, cols = part.shape
    inner = slice(BLOCK, cols - BLOCK)
    section = part[:, inner] + dot(high[...], halo[:, inner]) + dot(low[...], halo[:, inner])
    for b in range(BLOCK, cols - BLOCK, BLOCK):
        tile = slice(b, b + BLOCK)
        first = repeat_rows(speed[:levels, tile], rows // levels)
        second = repeat_rows(speed[levels:, tile], rows // levels)
        field = advance(section[:, b - BLOCK : b], first, second, wide, fine)
        field = 0.5 * (tr[:, tile] + field)
        warm = (0.5 * STEP) * heat[:, b - BLOCK : b]
        field = jnp.concatenate([field[:levels] + warm, field[levels:]], axis=0)
        own_high[:, tile], own_low[:, tile] = split(field)
    for start, value in zip(rim_starts(cols), (own_near, own_far), strict=True):
        tile = pl.ds(start, BLOCK)
        own_high[:, tile], own_low[:, tile] = split(value[...])
    out[...] = dot(own_high[...], local[...]) + dot(own_low[...], local[...])


def last_kernel(chunk, part, near, far, halo, heat_rim, heat_in, out_hbm, heat_hbm, out, sems):
    rows, cols = part.shape
    pairs = [
        (heat_rim.at[:, pl.ds(0, BLOCK)], heat_hbm.at[:, pl.ds(0, BLOCK)]),
        (heat_in, heat_hbm.at[:, pl.ds(BLOCK, cols - 2 * BLOCK)]),
        (heat_rim.at[:, pl.ds(BLOCK, BLOCK)], heat_hbm.at[:, pl.ds(cols - BLOCK, BLOCK)]),
    ]
    copies = [pltpu.make_async_copy(a, b, sems.at[k]) for k, (a, b) in enumerate(pairs)]
    for copy in copies:
        copy.start()
    whole_near, whole_far = decode(near[...]), decode(far[...])
    for k, r0 in enumerate(range(0, rows, chunk)):
        r = pl.ds(r0, chunk)
        high, low = halo_parts(whole_near[r0 : r0 + chunk], whole_far[r0 : r0 + chunk])
        out[r] = part[r] + dot(high, halo[...]) + dot(low, halo[...])
        copy = pltpu.make_async_copy(out.at[r], out_hbm.at[r], sems.at[len(pairs) + k])
        copy.start()
        copies.append(copy)
    for copy in copies:
        copy.wait()


def heat_kernel(blocks, first_call, after, absorber, cosine, mass, absorption, flux, lit, *refs):
    if first_call:
        out, weights, beams, depth = refs
    else:
        weights, beams, out, depth = refs
    gases, levels, points = absorption.shape
    width = len(blocks) * BLOCK
    span = gases * levels
    any_lit = jnp.max(lit[...])

    @pl.when(any_lit == 0)
    def _():
        out[...] = jnp.zeros_like(out)

    @pl.when(any_lit > 0)
    def _():
        if first_call:
            table = absorption[...].astype(F32).reshape(span, points).T
            keep = iota((levels, span), 1) % levels <= iota((levels, span), 0)
            for g in range(points):
                row = jnp.where(keep, table[g : g + 1], 0.0).astype(BF16)
                weights[g * levels : (g + 1) * levels] = row
            column = jnp.broadcast_to(flux[...], (8, points)).T[:, :1]
            beams[...] = jnp.broadcast_to(column, beams.shape)
        amounts = jnp.concatenate([absorber[b * BLOCK : (b + 1) * BLOCK] for b in blocks], axis=0)
        cos = jnp.concatenate([cosine[:, b * BLOCK : (b + 1) * BLOCK] for b in blocks], axis=1)
        cos = cos.astype(F32)
        scale = jnp.broadcast_to(-math.log2(math.e) / cos, (8, width))
        depth[...] = dot(weights[...], amounts.T)
        strips = range(0, levels, 8)
        tiles = range(0, width, BLOCK)
        totals = {(r, t): jnp.zeros((8, BLOCK), F32) for r in strips for t in tiles}
        for g in range(points):
            beam = jnp.broadcast_to(beams[g : g + 1], (8, BLOCK))
            for r, t in totals:
                d = depth[g * levels + r : g * levels + r + 8, t : t + BLOCK]
                totals[r, t] += beam * jnp.exp2(d * scale[:, t : t + BLOCK])
        down = [jnp.concatenate([totals[r, t] for r in strips], axis=0) for t in tiles]
        down = jnp.concatenate(down, axis=1)
        top = jnp.sum(beams[...], axis=0, keepdims=True)
        top = jnp.concatenate([top] * len(blocks), axis=1)
        above = jnp.concatenate([top, down[:-1]], axis=0)
        value = cos * (above - down)
        lanes = iota(lit.shape, 1)
        for k, b in enumerate(blocks):
            tile = slice(k * BLOCK, (k + 1) * BLOCK)
            on = jnp.sum(jnp.where(lanes == b, lit[...], 0), axis=1, keepdims=True).astype(F32)
            weight = mass[:, b * BLOCK : (b + 1) * BLOCK].astype(F32)
            out[:, tile] = on * value[:, tile] / weight


def struct(shape, dtype=F32):
    return pltpu.VMEM(shape, dtype)


def shards(
    tracers, velocity, metric, absorber, cosine, mass, absorption, flux, lit, neighbour, edge
):
    count, levels, cols = tracers.shape
    gases, points, _ = absorption.shape
    peers = lax.axis_size("sfc")
    total = neighbour.shape[1] * peers
    rows = count * levels
    pair = [(i, i ^ 1) for i in range(peers)]
    cross = [(i, (i + 2 * (i % 2) - 1) % peers) for i in range(peers)]
    tr = tracers.reshape(rows, cols)
    vel = velocity.reshape(2 * levels, cols)
    metric = metric.reshape(1, cols)
    absorption = absorption.transpose(0, 2, 1)
    flux = flux.reshape(1, points)
    lit = lit.reshape(1, -1)
    side = struct((rows, BLOCK))
    packed = struct((rows // 2 + 8, BLOCK), jnp.int32)
    half = struct((rows, 2 * BLOCK), BF16)
    full = struct((rows, cols))

    def like(x):
        return struct(x.shape, x.dtype)

    moved = (tr, vel, metric, neighbour, edge, absorber, mass, absorption, flux, lit, cosine)
    sent, far, wide, fine, *moved = pl.pallas_call(
        functools.partial(rim_kernel, levels),
        in_specs=[HBM] * len(moved),
        out_specs=[VMEM] * (4 + len(moved)),
        out_shape=[packed, side, struct((2 * BLOCK, 2 * BLOCK), BF16), struct((BLOCK, 2 * BLOCK), BF16)]
        + [like(x) for x in moved],
        scratch_shapes=[pltpu.SemaphoreType.DMA((len(moved) + 4,))],
        compiler_params=params(),
        name="rims_first",
    )(*[pltpu.with_memory_space_constraint(x, pltpu.HBM) for x in moved])
    tr, vel, metric, neighbour, edge, absorber, mass, absorption, flux, lit, cosine = moved
    cosine = cosine.reshape(1, cols)
    from_far = lax.ppermute(sent, "sfc", cross)
    weights = struct((points * levels, gases * levels), BF16)
    beams = struct((points, BLOCK))

    def heat(after, blocks, name, *extra):
        out = struct((levels, len(blocks) * BLOCK))
        return pl.pallas_call(
            functools.partial(heat_kernel, blocks, not extra),
            in_specs=[HBM] + [VMEM] * (6 + len(extra)),
            out_specs=VMEM if extra else [VMEM] * 3,
            out_shape=out if extra else [out, weights, beams],
            scratch_shapes=[pltpu.VMEM((points * levels, len(blocks) * BLOCK), F32)],
            compiler_params=params(16),
            cost_estimate=cost(1e9),
            name=name,
        )(after, absorber, cosine, mass, absorption, flux, lit, *extra)

    sent, part, speed, local, halo = pl.pallas_call(
        functools.partial(first_kernel, total, levels),
        in_specs=[VMEM] * 8,
        out_specs=[VMEM] * 5,
        out_shape=[
            packed,
            full,
            struct((2 * levels, cols)),
            struct((cols, cols), BF16),
            struct((2 * BLOCK, cols), BF16),
        ],
        scratch_shapes=[pltpu.VMEM((rows, cols), BF16)] * 2,
        compiler_params=params(),
        cost_estimate=cost(1e9),
        name="first_local",
    )(tr, vel, metric, wide, fine, far, neighbour, edge)
    from_near = lax.ppermute(sent, "sfc", pair)
    heat_rim, weights, beams = heat(halo, (0, 3), "heat_rims")

    own_sent, own_far, high, low = pl.pallas_call(
        functools.partial(far2_kernel, levels),
        in_specs=[VMEM] * 9,
        out_specs=[VMEM] * 4,
        out_shape=[packed, side, half, half],
        compiler_params=params(),
        name="far_second",
    )(part, from_near, from_far, halo, wide, fine, tr, speed, heat_rim)
    next_far = lax.ppermute(own_sent, "sfc", cross)
    own_sent, own_near = pl.pallas_call(
        functools.partial(near2_kernel, levels),
        in_specs=[VMEM] * 9,
        out_specs=[VMEM] * 2,
        out_shape=[packed, side],
        compiler_params=params(),
        name="near_second",
    )(part, high, low, halo, wide, fine, tr, speed, heat_rim)
    next_near = lax.ppermute(own_sent, "sfc", pair)
    heat_in = heat(high, (1, 2), "heat_inner", weights, beams)
    part2 = pl.pallas_call(
        functools.partial(inner2_kernel, levels),
        in_specs=[VMEM] * 12,
        out_specs=VMEM,
        out_shape=full,
        scratch_shapes=[pltpu.VMEM((rows, cols), BF16)] * 2,
        compiler_params=params(),
        cost_estimate=cost(1e9),
        name="second_local",
    )(part, high, low, halo, local, wide, fine, tr, speed, heat_in, own_near, own_far)
    advanced, heating = pl.pallas_call(
        functools.partial(last_kernel, 2 * levels),
        in_specs=[VMEM] * 6,
        out_specs=[HBM] * 2,
        out_shape=[jax.ShapeDtypeStruct((rows, cols), F32), jax.ShapeDtypeStruct((levels, cols), F32)],
        scratch_shapes=[pltpu.VMEM((rows, cols), F32), pltpu.SemaphoreType.DMA((3 + count // 2,))],
        compiler_params=params(),
        name="last",
    )(part2, next_near, next_far, halo, heat_rim, heat_in)
    return advanced.reshape(tracers.shape), heating


def solution(mesh):
    placed = (
        P(None, None, ("grp", "sfc")),
        P(None, None, ("grp", "sfc")),
        P(("grp", "sfc")),
        P(("grp", "sfc"), None),
        P(("grp", "sfc")),
        P(None, ("grp", "sfc")),
        P(),
        P(),
        P(("grp", "sfc")),
        P(None, ("grp", "sfc")),
        P(None, ("grp", "sfc")),
    )
    return jax.shard_map(
        shards,
        mesh=mesh,
        in_specs=placed,
        out_specs=(P(None, None, ("grp", "sfc")), P(None, ("grp", "sfc"))),
        check_vma=False,
    )
```

profile of v0, /device:TPU:0, one launch (start us, length us, event | category | flops | bytes accessed | tf_op | source)
XLA Modules:
  0.0 20.5 jit_solution(8525798579735663497)
XLA Ops:
  0.6 1.7 %rims_first.1 = (s32[264,128]{1,0:T(8,128)S(1)}, f32[512,128]{1,0:T(8,128)S(1)}, bf16[256,256]{1,0:T(8,128)(2,1)S(1)}, bf16[128,256]{1,0:T(8,128)(2,1)S(1)}, f32...) custom-call(f32[512,512]{1,0:T(8,128)} %bitcast.7, ...), custom_call_target="tpu_custom_call" | custom-call | tf_op jit(solution)/shard_map/rims_first/pallas_call | solution.py:404
  2.3 5.5 %collective-permute-start.1 = (s32[264,128]{1,0:T(8,128)S(1)}, s32[264,128]{1,0:T(8,128)S(1)}, u32[]{:S(2)}, u32[]{:S(2)}) collective-permute-start(s32[264,128]{1,0:T(8,128)S(1)} %get-tuple-element.43), channel_id=1, source_target_pairs={{0,15},{1,2},{2,1},{3,4},{4,3},{5,6},{6,5},{7,8},{8,7},{9,10},{10,... | collective-permute-start | bytes 405512 | tf_op jit(solution)/shard_map/ppermute | solution.py:416
  7.8 1.7 %first_local.1 = (s32[264,128]{1,0:T(8,128)S(1)}, f32[512,512]{1,0:T(8,128)S(1)}, f32[128,512]{1,0:T(8,128)S(1)}, bf16[512,512]{1,0:T(8,128)(2,1)S(1)}, bf16[256,512]{1,0:T(8,128)(2,1)S(1)}) custom-call(f32[512,512]{1,0:T(8,128)S(1)} %get-tuple-element.33.tr, f32[128,512]{1,0:T(8,128)S(1)} %get-tuple-element.34.vel, f32[1,512]{1,0:T(1,128)S(1)} %get-tuple-element.35.metric, ...), custom_call_target="tpu_custom_call" | custom-call | flops 1000000000 | bytes 1048576 | tf_op jit(solution)/shard_map/first_local/pallas_call | solution.py:433
  9.6 0.1 collective-permute-start
  9.7 0.2 %heat_rims.1 = (f32[64,256]{1,0:T(8,128)S(1)}, bf16[7168,256]{1,0:T(8,128)(2,1)S(1)}, f32[112,128]{1,0:T(8,128)S(1)}) custom-call(bf16[256,512]{1,0:T(8,128)(2,1)S(1)} %get-tuple-element.44.after.halo, bf16[512,256]{1,0:T(8,128)(2,1)S(1)} %get-tuple-element.46.absorber, bf16[1,512]{1,0:T(2,128)(2,1)S(1)} %reshape.30.cosine, ...), custom_call_target="tpu_custom_call" | custom-call | flops 1000000000 | bytes 1048576 | tf_op jit(solution)/shard_map/heat_rims/pallas_call | solution.py:422
  9.9 0.6 %collective-permute-done.1.sent = s32[264,128]{1,0:T(8,128)S(1)} collective-permute-done((s32[264,128]{1,0:T(8,128)S(1)}, s32[264,128]{1,0:T(8,128)S(1)}, u32[]{:S(2)}, u32[]{:S(2)}) %collective-permute-start.1) | collective-permute-done | bytes 135200 | tf_op jit(solution)/shard_map/ppermute | solution.py:416
  10.5 0.5 %collective-permute-done.near = s32[264,128]{1,0:T(8,128)S(1)} collective-permute-done((s32[264,128]{1,0:T(8,128)S(1)}, s32[264,128]{1,0:T(8,128)S(1)}, u32[]{:S(2)}, u32[]{:S(2)}) %collective-permute-start) | collective-permute-done | bytes 135200 | tf_op jit(solution)/shard_map/ppermute | solution.py:449
  11.0 1.0 %far_second.1 = (s32[264,128]{1,0:T(8,128)S(1)}, f32[512,128]{1,0:T(8,128)S(1)}, bf16[512,256]{1,0:T(8,128)(2,1)S(1)}, bf16[512,256]{1,0:T(8,128)(2,1)S(1)}) custom-call(f32[512,512]{1,0:T(8,128)S(1)} %get-tuple-element.41.part, s32[264,128]{1,0:T(8,128)S(1)} %collective-permute-done.near, s32[264,128]{1,0:T(8,128)S(1)} %collective-permute-done.1.sent, ...), custom_call_target="tpu_custom_call" | custom-call | tf_op jit(solution)/shard_map/far_second/pallas_call | solution.py:452
  12.0 4.0 %collective-permute-start.3 = (s32[264,128]{1,0:T(8,128)S(1)}, s32[264,128]{1,0:T(8,128)S(1)}, u32[]{:S(2)}, u32[]{:S(2)}) collective-permute-start(s32[264,128]{1,0:T(8,128)S(1)} %get-tuple-element.61), channel_id=1, source_target_pairs={{0,15},{1,2},{2,1},{3,4},{4,3},{5,6},{6,5},{7,8},{8,7},{9,10},{10,... | collective-permute-start | bytes 405512 | tf_op jit(solution)/shard_map/ppermute | solution.py:460
  16.0 0.9 %near_second.1 = (s32[264,128]{1,0:T(8,128)S(1)}, f32[512,128]{1,0:T(8,128)S(1)}) custom-call(f32[512,512]{1,0:T(8,128)S(1)} %get-tuple-element.41.part, bf16[512,256]{1,0:T(8,128)(2,1)S(1)} %get-tuple-element.53.after.high, bf16[512,256]{1,0:T(8,128)(2,1)S(1)} %get-tuple-element.54.low, bf16[256,512]{1,0:T(8,128)(2,1)S(1)} %get-tuple-element.44.after.halo, ...), custom_call_target="tpu_custom_call" | custom-call | tf_op jit(solution)/shard_map/near_second/pallas_call | solution.py:461
  16.9 0.1 collective-permute-start.2
  17.0 0.2 %heat_inner.1.heat.heat_in = f32[64,256]{1,0:T(8,128)S(1)} custom-call(bf16[512,256]{1,0:T(8,128)(2,1)S(1)} %get-tuple-element.53.after.high, bf16[512,256]{1,0:T(8,128)(2,1)S(1)} %get-tuple-element.46.absorber, bf16[1,512]{1,0:T(2,128)(2,1)S(1)} %reshape.30.cosine, bf16[64,512]{1,0:T(8,128)(2,1)S(1)} %get-tuple-element.48.mass, ...), custom_call_target="tpu_custom_call" | custom-call | flops 1000000000 | bytes 1048576 | tf_op jit(solution)/shard_map/heat_inner/pallas_call | solution.py:422
  17.2 1.7 %second_local.1.part = f32[512,512]{1,0:T(8,128)S(1)} custom-call(f32[512,512]{1,0:T(8,128)S(1)} %get-tuple-element.41.part, bf16[512,256]{1,0:T(8,128)(2,1)S(1)} %get-tuple-element.53.after.high, bf16[512,256]{1,0:T(8,128)(2,1)S(1)} %get-tuple-element.54.low, bf16[256,512]{1,0:T(8,128)(2,1)S(1)} %get-tuple-element.44.after.halo, ...), custom_call_target="tpu_custom_call" | custom-call | flops 1000000000 | bytes 1048576 | tf_op jit(solution)/shard_map/second_local/pallas_call | solution.py:471
  18.9 0.3 %collective-permute-done.3.far = s32[264,128]{1,0:T(8,128)S(1)} collective-permute-done((s32[264,128]{1,0:T(8,128)S(1)}, s32[264,128]{1,0:T(8,128)S(1)}, u32[]{:S(2)}, u32[]{:S(2)}) %collective-permute-start.3) | collective-permute-done | bytes 135200 | tf_op jit(solution)/shard_map/ppermute | solution.py:460
  19.2 0.0 collective-permute-done.2.near
  19.2 1.3 %last.1 = (f32[512,512]{1,0:T(8,128)}, f32[64,512]{1,0:T(8,128)}) custom-call(f32[512,512]{1,0:T(8,128)S(1)} %second_local.1.part, s32[264,128]{1,0:T(8,128)S(1)} %collective-permute-done.2.near, s32[264,128]{1,0:T(8,128)S(1)} %collective-permute-done.3.far, bf16[256,512]{1,0:T(8,128)(2,1)S(1)} %get-tuple-element.44.after.halo, ...), custom_call_target="tpu_custom_call" | custom-call | tf_op jit(solution)/shard_map/last/pallas_call | solution.py:481
  (1 shorter events, 0.0 us)
Async XLA Ops:
  2.3 8.2 %collective-permute-start.1 = (s32[264,128]{1,0:T(8,128)S(1)}, s32[264,128]{1,0:T(8,128)S(1)}, u32[]{:S(2)}, u32[]{:S(2)}) collective-permute-start(s32[264,128]{1,0:T(8,128)S(1)} %get-tuple-element.43), channel_id=1, source_target_pairs={{0,15},{1,2},{2,1},{3,4},{4,3},{5,6},{6,5},{7,8},{8,7},{9,10},{10,... | collective-permute-start | bytes 405512 | tf_op jit(solution)/shard_map/ppermute | solution.py:416
  9.6 1.4 %collective-permute-start = (s32[264,128]{1,0:T(8,128)S(1)}, s32[264,128]{1,0:T(8,128)S(1)}, u32[]{:S(2)}, u32[]{:S(2)}) collective-permute-start(s32[264,128]{1,0:T(8,128)S(1)} %get-tuple-element.42), channel_id=1, source_target_pairs={{0,1},{1,0},{2,3},{3,2},{4,5},{5,4},{6,7},{7,6},{8,9},{9,8},{10,11... | collective-permute-start | bytes 405512 | tf_op jit(solution)/shard_map/ppermute | solution.py:449
  12.0 7.2 %collective-permute-start.3 = (s32[264,128]{1,0:T(8,128)S(1)}, s32[264,128]{1,0:T(8,128)S(1)}, u32[]{:S(2)}, u32[]{:S(2)}) collective-permute-start(s32[264,128]{1,0:T(8,128)S(1)} %get-tuple-element.61), channel_id=1, source_target_pairs={{0,15},{1,2},{2,1},{3,4},{4,3},{5,6},{6,5},{7,8},{8,7},{9,10},{10,... | collective-permute-start | bytes 405512 | tf_op jit(solution)/shard_map/ppermute | solution.py:460
  16.9 2.3 %collective-permute-start.2 = (s32[264,128]{1,0:T(8,128)S(1)}, s32[264,128]{1,0:T(8,128)S(1)}, u32[]{:S(2)}, u32[]{:S(2)}) collective-permute-start(s32[264,128]{1,0:T(8,128)S(1)} %get-tuple-element.60), channel_id=1, source_target_pairs={{0,1},{1,0},{2,3},{3,2},{4,5},{5,4},{6,7},{7,6},{8,9},{9,8},{10,11... | collective-permute-start | bytes 405512 | tf_op jit(solution)/shard_map/ppermute | solution.py:469
where the time goes:
time: 20.7 us; the launch traced here: 20.5 us
  starting transfers between devices  9.69 us (47%)
  Pallas kernels  8.68 us (42%)
  waiting for transfers between devices  1.42 us (7%)
  between operations  0.71 us (3%)
    ppermute x1, starting transfers between devices, shards(): from_far = lax.ppermute(sent, 'sfc', cross)  5.51 us
    ppermute x1, starting transfers between devices, shards(): next_far = lax.ppermute(own_sent, 'sfc', cross)  4.03 us
    pallas_call x1, Pallas kernels, shards(): pl.pallas_call(functools.partial(first_kernel, total, levels), in_specs=[...  1.74 us
    pallas_call x1, Pallas kernels, shards(): pl.pallas_call(functools.partial(rim_kernel, levels), in_specs=[HBM] * le...  1.67 us
    pallas_call x1, Pallas kernels, shards(): pl.pallas_call(functools.partial(inner2_kernel, levels), in_specs=[VMEM]...  1.65 us
    pallas_call x1, Pallas kernels, shards(): pl.pallas_call(functools.partial(last_kernel, 2 * levels), in_specs=[VMEM...  1.3 us
    pallas_call x1, Pallas kernels, shards(): pl.pallas_call(functools.partial(far2_kernel, levels), in_specs=[VMEM] *...  1 us
    pallas_call x1, Pallas kernels, shards(): pl.pallas_call(functools.partial(near2_kernel, levels), in_specs=[VMEM] *...  0.89 us
  transfers between devices with their start and end apart: 4, of which 3 were waited for; matrix products, arithmetic and copies ran while one was open for 0% of the time, Pallas kernels for 23%

commit v1 on v0

--- a/solution.py
+++ b/solution.py
@@ -151,7 +151,7 @@
     packed = pack(rim)
     strips = [packed[r : r + 8] for r in range(0, packed.shape[0], 8)]
     largest = functools.reduce(jnp.maximum, [jnp.abs(x) for x in strips])
-    power = jnp.clip(jnp.ceil(jnp.log2(largest)), -125.0, 125.0)
+    power = jnp.clip(jnp.ceil(jnp.log2(largest) + 1e-3), -125.0, 125.0)
     scale = jnp.exp2(-power)
     count = len(strips) // 3
     words = [(x * scale * SPAN + (HALF + 0.5)).astype(jnp.int32) for x in strips]

time: 20.7 us -> 21.8 us (1.053)
  Pallas kernels: 8.68 us -> 11.8 us
  waiting for transfers between devices: 1.42 us -> 0.01 us
  starting transfers between devices: 9.69 us -> 9.07 us
    pallas_call x2, Pallas kernels: 0.42 us -> 3.54 us  [heat(): pl.pallas_call(functools.partial(heat_kernel, blocks, not extra), in_spec...]
    ppermute x1, waiting for transfers between devices: 0.64 us -> 0.01 us  [shards(): from_far = lax.ppermute(sent, 'sfc', cross)]
    ppermute x1, starting transfers between devices: 4.03 us -> 3.42 us  [shards(): next_far = lax.ppermute(own_sent, 'sfc', cross)]
    ppermute x1, waiting for transfers between devices: 0.47 us -> 0.01 us  [shards(): from_near = lax.ppermute(sent, 'sfc', pair)]
    ppermute x1, waiting for transfers between devices: 0.31 us -> 0.01 us  [shards(): next_far = lax.ppermute(own_sent, 'sfc', cross)]
  transfers between devices with their start and end apart: 4 -> 4, of which waited for: 3 -> 0; matrix products, arithmetic and copies ran while one was open for 0% -> 0% of each run, Pallas kernels for 23% -> 36%
where the time goes in v1:
time: 21.8 us; the launch traced here: 21.6 us
  Pallas kernels  11.8 us (54%)
  starting transfers between devices  9.07 us (42%)
  between operations  0.74 us (3%)
    ppermute x1, starting transfers between devices, shards(): from_far = lax.ppermute(sent, 'sfc', cross)  5.51 us
    pallas_call x2, Pallas kernels, heat(): pl.pallas_call(functools.partial(heat_kernel, blocks, not extra), in_spec...  3.54 us
    ppermute x1, starting transfers between devices, shards(): next_far = lax.ppermute(own_sent, 'sfc', cross)  3.42 us
    pallas_call x1, Pallas kernels, shards(): pl.pallas_call(functools.partial(first_kernel, total, levels), in_specs=[...  1.75 us
    pallas_call x1, Pallas kernels, shards(): pl.pallas_call(functools.partial(rim_kernel, levels), in_specs=[HBM] * le...  1.66 us
    pallas_call x1, Pallas kernels, shards(): pl.pallas_call(functools.partial(inner2_kernel, levels), in_specs=[VMEM]...  1.65 us
    pallas_call x1, Pallas kernels, shards(): pl.pallas_call(functools.partial(last_kernel, 2 * levels), in_specs=[VMEM...  1.3 us
    pallas_call x1, Pallas kernels, shards(): pl.pallas_call(functools.partial(far2_kernel, levels), in_specs=[VMEM] *...  1.01 us
  transfers between devices with their start and end apart: 4, of which 0 were waited for; matrix products, arithmetic and copies ran while one was open for 0% of the time, Pallas kernels for 36%

profile of v1, /device:TPU:0, one launch (start us, length us, event | category | flops | bytes accessed | tf_op | source)
XLA Modules:
  0.0 21.6 jit_solution(14520297164117770219)
XLA Ops:
  0.6 1.7 %rims_first.1 = (s32[264,128]{1,0:T(8,128)S(1)}, f32[512,128]{1,0:T(8,128)S(1)}, bf16[256,256]{1,0:T(8,128)(2,1)S(1)}, bf16[128,256]{1,0:T(8,128)(2,1)S(1)}, f32...) custom-call(f32[512,512]{1,0:T(8,128)} %bitcast.7, ...), custom_call_target="tpu_custom_call" | custom-call | tf_op jit(solution)/shard_map/rims_first/pallas_call | solution.py:404
  2.3 5.5 %collective-permute-start.1 = (s32[264,128]{1,0:T(8,128)S(1)}, s32[264,128]{1,0:T(8,128)S(1)}, u32[]{:S(2)}, u32[]{:S(2)}) collective-permute-start(s32[264,128]{1,0:T(8,128)S(1)} %get-tuple-element.43), channel_id=1, source_target_pairs={{0,15},{1,2},{2,1},{3,4},{4,3},{5,6},{6,5},{7,8},{8,7},{9,10},{10,... | collective-permute-start | bytes 405512 | tf_op jit(solution)/shard_map/ppermute | solution.py:416
  7.8 1.8 %first_local.1 = (s32[264,128]{1,0:T(8,128)S(1)}, f32[512,512]{1,0:T(8,128)S(1)}, f32[128,512]{1,0:T(8,128)S(1)}, bf16[512,512]{1,0:T(8,128)(2,1)S(1)}, bf16[256,512]{1,0:T(8,128)(2,1)S(1)}) custom-call(f32[512,512]{1,0:T(8,128)S(1)} %get-tuple-element.33.tr, f32[128,512]{1,0:T(8,128)S(1)} %get-tuple-element.34.vel, f32[1,512]{1,0:T(1,128)S(1)} %get-tuple-element.35.metric, ...), custom_call_target="tpu_custom_call" | custom-call | flops 1000000000 | bytes 1048576 | tf_op jit(solution)/shard_map/first_local/pallas_call | solution.py:433
  9.6 0.1 collective-permute-start
  9.7 1.9 %heat_rims.1 = (f32[64,256]{1,0:T(8,128)S(1)}, bf16[7168,256]{1,0:T(8,128)(2,1)S(1)}, f32[112,128]{1,0:T(8,128)S(1)}) custom-call(bf16[256,512]{1,0:T(8,128)(2,1)S(1)} %get-tuple-element.44.after.halo, bf16[512,256]{1,0:T(8,128)(2,1)S(1)} %get-tuple-element.46.absorber, bf16[1,512]{1,0:T(2,128)(2,1)S(1)} %reshape.30.cosine, ...), custom_call_target="tpu_custom_call" | custom-call | flops 1000000000 | bytes 1048576 | tf_op jit(solution)/shard_map/heat_rims/pallas_call | solution.py:422
  11.6 0.0 collective-permute-done.1.sent
  11.6 0.0 collective-permute-done.near
  11.6 1.0 %far_second.1 = (s32[264,128]{1,0:T(8,128)S(1)}, f32[512,128]{1,0:T(8,128)S(1)}, bf16[512,256]{1,0:T(8,128)(2,1)S(1)}, bf16[512,256]{1,0:T(8,128)(2,1)S(1)}) custom-call(f32[512,512]{1,0:T(8,128)S(1)} %get-tuple-element.41.part, s32[264,128]{1,0:T(8,128)S(1)} %collective-permute-done.near, s32[264,128]{1,0:T(8,128)S(1)} %collective-permute-done.1.sent, ...), custom_call_target="tpu_custom_call" | custom-call | tf_op jit(solution)/shard_map/far_second/pallas_call | solution.py:452
  12.6 3.4 %collective-permute-start.3 = (s32[264,128]{1,0:T(8,128)S(1)}, s32[264,128]{1,0:T(8,128)S(1)}, u32[]{:S(2)}, u32[]{:S(2)}) collective-permute-start(s32[264,128]{1,0:T(8,128)S(1)} %get-tuple-element.61), channel_id=1, source_target_pairs={{0,15},{1,2},{2,1},{3,4},{4,3},{5,6},{6,5},{7,8},{8,7},{9,10},{10,... | collective-permute-start | bytes 405512 | tf_op jit(solution)/shard_map/ppermute | solution.py:460
  16.0 0.9 %near_second.1 = (s32[264,128]{1,0:T(8,128)S(1)}, f32[512,128]{1,0:T(8,128)S(1)}) custom-call(f32[512,512]{1,0:T(8,128)S(1)} %get-tuple-element.41.part, bf16[512,256]{1,0:T(8,128)(2,1)S(1)} %get-tuple-element.53.after.high, bf16[512,256]{1,0:T(8,128)(2,1)S(1)} %get-tuple-element.54.low, bf16[256,512]{1,0:T(8,128)(2,1)S(1)} %get-tuple-element.44.after.halo, ...), custom_call_target="tpu_custom_call" | custom-call | tf_op jit(solution)/shard_map/near_second/pallas_call | solution.py:461
  16.9 0.1 collective-permute-start.2
  17.0 1.6 %heat_inner.1.heat.heat_in = f32[64,256]{1,0:T(8,128)S(1)} custom-call(bf16[512,256]{1,0:T(8,128)(2,1)S(1)} %get-tuple-element.53.after.high, bf16[512,256]{1,0:T(8,128)(2,1)S(1)} %get-tuple-element.46.absorber, bf16[1,512]{1,0:T(2,128)(2,1)S(1)} %reshape.30.cosine, bf16[64,512]{1,0:T(8,128)(2,1)S(1)} %get-tuple-element.48.mass, ...), custom_call_target="tpu_custom_call" | custom-call | flops 1000000000 | bytes 1048576 | tf_op jit(solution)/shard_map/heat_inner/pallas_call | solution.py:422
  18.6 1.7 %second_local.1.part = f32[512,512]{1,0:T(8,128)S(1)} custom-call(f32[512,512]{1,0:T(8,128)S(1)} %get-tuple-element.41.part, bf16[512,256]{1,0:T(8,128)(2,1)S(1)} %get-tuple-element.53.after.high, bf16[512,256]{1,0:T(8,128)(2,1)S(1)} %get-tuple-element.54.low, bf16[256,512]{1,0:T(8,128)(2,1)S(1)} %get-tuple-element.44.after.halo, ...), custom_call_target="tpu_custom_call" | custom-call | flops 1000000000 | bytes 1048576 | tf_op jit(solution)/shard_map/second_local/pallas_call | solution.py:471
  20.3 0.0 collective-permute-done.3.far
  20.3 0.0 collective-permute-done.2.near
  20.3 1.3 %last.1 = (f32[512,512]{1,0:T(8,128)}, f32[64,512]{1,0:T(8,128)}) custom-call(f32[512,512]{1,0:T(8,128)S(1)} %second_local.1.part, s32[264,128]{1,0:T(8,128)S(1)} %collective-permute-done.2.near, s32[264,128]{1,0:T(8,128)S(1)} %collective-permute-done.3.far, bf16[256,512]{1,0:T(8,128)(2,1)S(1)} %get-tuple-element.44.after.halo, ...), custom_call_target="tpu_custom_call" | custom-call | tf_op jit(solution)/shard_map/last/pallas_call | solution.py:481
  (1 shorter events, 0.0 us)
Async XLA Ops:
  2.3 9.3 %collective-permute-start.1 = (s32[264,128]{1,0:T(8,128)S(1)}, s32[264,128]{1,0:T(8,128)S(1)}, u32[]{:S(2)}, u32[]{:S(2)}) collective-permute-start(s32[264,128]{1,0:T(8,128)S(1)} %get-tuple-element.43), channel_id=1, source_target_pairs={{0,15},{1,2},{2,1},{3,4},{4,3},{5,6},{6,5},{7,8},{8,7},{9,10},{10,... | collective-permute-start | bytes 405512 | tf_op jit(solution)/shard_map/ppermute | solution.py:416
  9.6 2.0 %collective-permute-start = (s32[264,128]{1,0:T(8,128)S(1)}, s32[264,128]{1,0:T(8,128)S(1)}, u32[]{:S(2)}, u32[]{:S(2)}) collective-permute-start(s32[264,128]{1,0:T(8,128)S(1)} %get-tuple-element.42), channel_id=1, source_target_pairs={{0,1},{1,0},{2,3},{3,2},{4,5},{5,4},{6,7},{7,6},{8,9},{9,8},{10,11... | collective-permute-start | bytes 405512 | tf_op jit(solution)/shard_map/ppermute | solution.py:449
  12.6 7.7 %collective-permute-start.3 = (s32[264,128]{1,0:T(8,128)S(1)}, s32[264,128]{1,0:T(8,128)S(1)}, u32[]{:S(2)}, u32[]{:S(2)}) collective-permute-start(s32[264,128]{1,0:T(8,128)S(1)} %get-tuple-element.61), channel_id=1, source_target_pairs={{0,15},{1,2},{2,1},{3,4},{4,3},{5,6},{6,5},{7,8},{8,7},{9,10},{10,... | collective-permute-start | bytes 405512 | tf_op jit(solution)/shard_map/ppermute | solution.py:460
  16.9 3.4 %collective-permute-start.2 = (s32[264,128]{1,0:T(8,128)S(1)}, s32[264,128]{1,0:T(8,128)S(1)}, u32[]{:S(2)}, u32[]{:S(2)}) collective-permute-start(s32[264,128]{1,0:T(8,128)S(1)} %get-tuple-element.60), channel_id=1, source_target_pairs={{0,1},{1,0},{2,3},{3,2},{4,5},{5,4},{6,7},{7,6},{8,9},{9,8},{10,11... | collective-permute-start | bytes 405512 | tf_op jit(solution)/shard_map/ppermute | solution.py:469
